TPU v7x, 256 devices: a whole 4x4x8 slice. The times are simulated.
256 devices in a mesh: beam: 2 (over x_lo), row: 2 (over core), col: 64 (over z, y, x_hi).
Axes of the slice: x: 4 (x_hi: 2, x_lo: 2; x = x_hi * 2 + x_lo), y: 4, z: 8, core: 2. Of those that a mesh axis runs over, the one named last changes fastest.
Arguments:
- transmission: float32 [2, 2, 512, 16384], P(None, 'beam', 'row', 'col')
- probe_field: float32 [2, 256, 256], replicated, may hold values from -4.2 to 4.2
- propagator: float32 [2, 256, 256], replicated
- intensities: float32 [256, 256, 256], P(('row', 'col')), may hold values from 0 to 3
- positions: int32 [256, 2], P(('row', 'col')), may hold values from 128 to 16256, as said below
- live_slots: int32 [256], P(('row', 'col')), may hold values from 0 to 1, as said below
Outputs:
- gradient: float32 [2, 2, 512, 16384], P(None, 'beam', 'row', 'col')
Inputs may be any that keep to these rules, and one draw needn't show every extreme that they name: `positions`: each probe's center lies in the lateral tile of 256 x 256 cells of the device that holds its slot, and its footprint of 256 x 256 cells lies inside the object. `live_slots`: 1 marks a probe of the batch, 0 an empty slot; on each device the live slots come first, each device has one or more, and some device has all 2 live.
All inputs are finite; a program needn't handle non-finite values.
Results may differ from a plain program's by a relative error of at most 0.0003.
Values sent between devices are 32-bit elements; how exact they have to be, the bound alone decides.
A program may use at most 64 MiB of HBM per device.

v0:
```python
import functools

import jax
import jax.numpy as jnp
import numpy as np
from jax import lax
from jax.experimental import pallas as pl
from jax.experimental.pallas import tpu as pltpu
from jax.sharding import PartitionSpec as P

MESH = pl.DeviceIdType.MESH
SIDE = 256
HALF = 128
F32 = jnp.float32
BF16 = jnp.bfloat16

TILE = 0
LEFTWARD = 4
RIGHTWARD = 6
RELAY_RIGHT = 8
RELAY_BEAM = 10
ROW = 12
GRAD_ROW = 20
GRAD_COL = 24
COPIES = 28


def transform_table(side):
    counter = np.arange(side)
    angles = 2.0 * np.pi / side * (counter[:, None] * counter[None, :] % side)
    return np.stack([np.cos(angles), -np.sin(angles)]).astype(np.float32) / np.float32(np.sqrt(side))


def split(value):
    high = value.astype(BF16)
    return high, (value - high.astype(F32)).astype(BF16)


def put_operator(operators, at, real, imag):
    real_high, real_low = split(real)
    imag_high, imag_low = split(imag)
    top = (real_high, real_high, real_low, -imag_high, -imag_high, -imag_low)
    low = (imag_high, imag_high, imag_low, real_high, real_high, real_low)
    for block in range(6):
        columns = slice(block * SIDE, (block + 1) * SIDE)
        operators[at, :SIDE, columns] = top[block]
        operators[at, SIDE:, columns] = low[block]


def kernel(
    cols,
    pos,
    live,
    trans,
    probe_hbm,
    prop_hbm,
    table_hbm,
    intens_hbm,
    out,
    ext,
    probe,
    prop,
    table,
    intens,
    operators,
    parts,
    wave,
    psi,
    window,
    pad,
    grad,
    grad_rows,
    grad_cols,
    local_sem,
    send_sem,
    recv_sem,
):
    beam, row, col = lax.axis_index("beam"), lax.axis_index("row"), lax.axis_index("col")
    other = 1 - beam
    has_left, has_right = col > 0, col < cols - 1
    partner = (other, row, col)
    sibling = (beam, 1 - row, col)
    left = (other, row, jnp.maximum(col - 1, 0))
    right = (other, row, jnp.minimum(col + 1, cols - 1))

    barrier = pltpu.get_barrier_semaphore()

    def greet(peer):
        pl.semaphore_signal(barrier, inc=1, device_id=peer, device_id_type=MESH)

    greet(partner)
    greet(sibling)
    pl.when(has_left)(lambda: greet(left))
    pl.when(has_right)(lambda: greet(right))

    def rows(start):
        return pl.ds(pl.multiple_of(start, HALF), HALF)

    tile_rows = (rows(HALF * (1 - row)), rows(HALF * row))
    ext_rows = (rows(jnp.int32(HALF)), rows(2 * HALF * row))
    sibling_rows = rows(2 * HALF * row)

    locals_ = [
        pltpu.make_async_copy(
            trans.at[:, 0, :, pl.ds(HALF * k, HALF)],
            ext.at[beam, 1 + k, :, pl.ds(pl.multiple_of(HALF * row, HALF), SIDE), :],
            local_sem.at[k],
        )
        for k in range(2)
    ]
    for at, (source, target) in enumerate(
        ((prop_hbm, prop), (table_hbm, table), (probe_hbm, probe), (intens_hbm, intens))
    ):
        locals_.append(pltpu.make_async_copy(source, target, local_sem.at[2 + at]))
    for copy in locals_:
        copy.start()

    def remote(at, source, target, peer):
        return pltpu.make_async_remote_copy(
            src_ref=source,
            dst_ref=target,
            send_sem=send_sem.at[at],
            recv_sem=recv_sem.at[at],
            device_id=peer,
            device_id_type=MESH,
        )

    def own(k, h):
        return trans.at[:, 0, tile_rows[h], pl.ds(HALF * k, HALF)]

    def block(of, k, h):
        return ext.at[of, k, :, ext_rows[h], :]

    tile = [[remote(TILE + 2 * k + h, own(k, h), block(beam, 1 + k, h), partner) for h in range(2)] for k in range(2)]
    leftward = [remote(LEFTWARD + h, own(0, h), block(beam, 3, h), left) for h in range(2)]
    rightward = [remote(RIGHTWARD + h, own(1, h), block(beam, 0, h), right) for h in range(2)]
    relay_right = [remote(RELAY_RIGHT + h, block(other, 2, h), block(other, 0, h), right) for h in range(2)]
    relay_beam = [remote(RELAY_BEAM + h, block(other, 3, h), block(other, 3, h), partner) for h in range(2)]

    def to_sibling(at, of, k, source=None):
        return remote(
            ROW + at, block(of, k, 0) if source is None else source, ext.at[of, k, :, sibling_rows, :], sibling
        )

    row_own = [to_sibling(k, beam, 1 + k, own(k, 0)) for k in range(2)]
    row_other = [to_sibling(2 + k, other, 1 + k) for k in range(2)]
    row_left_other = to_sibling(4, other, 0)
    row_left_own = to_sibling(5, beam, 0)
    row_right_other = to_sibling(6, other, 3)
    row_right_own = to_sibling(7, beam, 3)

    pl.semaphore_wait(barrier, 2 + jnp.where(has_left, 1, 0) + jnp.where(has_right, 1, 0))

    for h in range(2):
        tile[1][h].start()
        pl.when(has_left)(leftward[h].start)
    for h in range(2):
        tile[0][h].start()
        pl.when(has_right)(rightward[h].start)
    for k in range(2):
        row_own[k].start()

    for copy in locals_:
        copy.wait()
    put_operator(operators, 0, prop[0], prop[1])
    put_operator(operators, 1, prop[0].T, -prop[1].T)

    def then(copy, *followers):
        copy.wait_recv()
        for follower in followers:
            follower.start()

    def tile_right(h):
        tile[1][h].wait_recv()
        pl.when(has_right)(relay_right[h].start)
        if h == 0:
            row_other[1].start()

    def from_right(h):
        then(leftward[h], relay_beam[h], *((row_right_other,) if h == 0 else ()))

    for h in range(2):
        tile_right(h)
        pl.when(has_right)(functools.partial(from_right, h))

    put_operator(operators, 2, table[0], table[1])
    put_operator(operators, 3, table[0], -table[1])
    edge = jnp.zeros((2, 4 * HALF, HALF), F32)
    strip = jnp.zeros((2, HALF, HALF), F32)
    for slot in range(2):
        pad[slot, 0] = edge
        pad[slot, 4] = edge
        for k in range(1, 4):
            pad[slot, k, :, :HALF] = strip
            pad[slot, k, :, 3 * HALF :] = strip

    side_zero = jnp.zeros((2, 2, 3 * HALF, HALF), F32)

    @pl.when(jnp.logical_not(has_left))
    def _():
        ext[:, 0] = side_zero

    @pl.when(jnp.logical_not(has_right))
    def _():
        ext[:, 3] = side_zero

    then(tile[0][0], row_other[0])

    @pl.when(has_left)
    def _():
        then(rightward[0], row_left_other)

    then(tile[0][1])

    @pl.when(has_left)
    def _():
        then(rightward[1])
        then(relay_right[0], row_left_own)

    @pl.when(has_right)
    def _():
        then(relay_beam[0], row_right_own)

    @pl.when(has_left)
    def _():
        relay_right[1].wait_recv()

    @pl.when(has_right)
    def _():
        relay_beam[1].wait_recv()

    for k in range(2):
        row_own[k].wait_recv()
        row_other[k].wait_recv()

    @pl.when(has_left)
    def _():
        row_left_other.wait_recv()
        row_left_own.wait_recv()

    @pl.when(has_right)
    def _():
        row_right_other.wait_recv()
        row_right_own.wait_recv()

    row_at = [jnp.clip(pos[slot, 0] - HALF - HALF * row, 0, HALF) for slot in range(2)]
    col_at = [jnp.clip(pos[slot, 1] - SIDE * col, 0, SIDE - 1) for slot in range(2)]
    block_at = [at // HALF for at in col_at]
    lane_at = [at % HALF for at in col_at]
    lanes = lax.broadcasted_iota(jnp.int32, (SIDE, HALF), 1)

    def footprint(of, slot, part):
        back = lax.rem(HALF - lane_at[slot], HALF)
        turned = [
            pltpu.roll(ext[of, block_at[slot] + j, part, pl.ds(row_at[slot], SIDE), :], back, 1) for j in range(3)
        ]
        near = lanes < HALF - lane_at[slot]
        return [jnp.where(near, turned[j], turned[j + 1]) for j in range(2)]

    def spread(operator):
        def stage(counter, carry):
            for slot in range(2):
                for part in range(2):
                    high, low = split(wave[slot, SIDE * part : SIDE * (part + 1)])
                    start = 3 * SIDE * part
                    parts[slot, :, start : start + SIDE] = high
                    parts[slot, :, start + SIDE : start + 2 * SIDE] = low
                    parts[slot, :, start + 2 * SIDE : start + 3 * SIDE] = high
                wave[slot] = lax.dot_general(
                    operators[operator], parts[slot], (((1,), (1,)), ((), ())), preferred_element_type=F32
                )
            return carry

        lax.fori_loop(0, 2, stage, 0)

    real, imag = slice(0, SIDE), slice(SIDE, 2 * SIDE)

    for slot in range(2):
        window_real, window_imag = footprint(0, slot, 0), footprint(0, slot, 1)
        for j in range(2):
            at = slice(j * HALF, (j + 1) * HALF)
            probe_real, probe_imag = probe[0, :, at], probe[1, :, at]
            wave[slot, real, at] = window_real[j] * probe_real - window_imag[j] * probe_imag
            wave[slot, imag, at] = window_real[j] * probe_imag + window_imag[j] * probe_real
    spread(0)
    for slot in range(2):
        window_real, window_imag = footprint(1, slot, 0), footprint(1, slot, 1)
        for j in range(2):
            at = slice(j * HALF, (j + 1) * HALF)
            wave_real, wave_imag = wave[slot, real, at], wave[slot, imag, at]
            psi[slot, real, at], psi[slot, imag, at] = wave_real, wave_imag
            window[slot, real, at], window[slot, imag, at] = window_real[j], window_imag[j]
            wave[slot, real, at] = window_real[j] * wave_real - window_imag[j] * wave_imag
            wave[slot, imag, at] = window_real[j] * wave_imag + window_imag[j] * wave_real
    spread(0)
    spread(2)
    for slot in range(2):
        far_real, far_imag = wave[slot, real], wave[slot, imag]
        weight = live[slot].astype(F32)
        residual = weight * (far_real * far_real + far_imag * far_imag - intens[slot])
        wave[slot, real] = residual * far_real
        wave[slot, imag] = residual * far_imag
    spread(3)
    spread(1)

    middle = slice(HALF, 3 * HALF)

    def place(slot, part, pieces):
        turned = [pltpu.roll(piece, lane_at[slot], 1) for piece in pieces]
        inside = lanes >= lane_at[slot]
        zero = jnp.zeros_like(turned[0])
        pad[slot, 1, part, middle] = jnp.where(inside, turned[0], zero)
        pad[slot, 2, part, middle] = jnp.where(inside, turned[1], turned[0])
        pad[slot, 3, part, middle] = jnp.where(inside, zero, turned[1])

    def collect(of):
        core = jnp.where(beam == of, 1, 0)
        for side in range(2):
            at = jnp.where(beam == of, 1 + side, 3 * side)
            for part in range(2):
                terms = [
                    pad[slot, at + 1 - block_at[slot], part, pl.ds(HALF - row_at[slot], 3 * HALF), :]
                    for slot in range(2)
                ]
                grad[core, side, part] = terms[0] + terms[1]

    def gradient(slot, lit_real, lit_imag):
        pieces = ([], [])
        for j in range(2):
            at = slice(j * HALF, (j + 1) * HALF)
            back_real, back_imag = wave[slot, real, at], wave[slot, imag, at]
            first, second = lit_real(at), lit_imag(at)
            pieces[0].append(first * back_real + second * back_imag)
            pieces[1].append(first * back_imag - second * back_real)
        place(slot, 0, pieces[0])
        place(slot, 1, pieces[1])

    away_rows = rows(2 * HALF * (1 - row))
    grad_row = [
        [
            remote(GRAD_ROW + 2 * core + side, grad.at[core, side, :, away_rows, :], grad_rows.at[core, side], sibling)
            for side in range(2)
        ]
        for core in range(2)
    ]
    grad_col = [
        [
            remote(
                GRAD_COL + 2 * side + h,
                grad.at[0, side, :, ext_rows[h], :],
                grad_cols.at[side, h],
                right if side else left,
            )
            for h in range(2)
        ]
        for side in range(2)
    ]
    has_side = (has_left, has_right)

    def send_halo():
        for side in range(2):
            grad_row[0][side].start()
            pl.when(has_side[side])(grad_col[side][1].start)

    for slot in range(2):
        gradient(slot, lambda at: psi[slot, real, at], lambda at: psi[slot, imag, at])
        back_real, back_imag = wave[slot, real], wave[slot, imag]
        window_real, window_imag = window[slot, real], window[slot, imag]
        wave[slot, real] = window_real * back_real + window_imag * back_imag
        wave[slot, imag] = window_real * back_imag - window_imag * back_real
    collect(1)
    pl.when(beam == 0)(send_halo)
    spread(1)
    for slot in range(2):
        gradient(slot, lambda at: probe[0, :, at], lambda at: probe[1, :, at])
    collect(0)
    pl.when(beam == 1)(send_halo)
    for side in range(2):
        grad_row[1][side].start()
    for side in range(2):
        grad_row[0][side].wait_recv()

        @pl.when(has_side[side])
        def _():
            grad[0, side, :, HALF : 2 * HALF] += grad_rows[0, side]
            grad_col[side][0].start()

    for side in range(2):
        at = slice(side * HALF, (side + 1) * HALF)
        grad_row[1][side].wait_recv()
        out[:, 0, tile_rows[0], at] = grad[1, side, :, HALF : 2 * HALF] + grad_rows[1, side]
        out[:, 0, tile_rows[1], at] = grad[1, side, :, ext_rows[1]]
    for h in (1, 0):
        for side in range(2):
            at = slice(side * HALF, (side + 1) * HALF)

            @pl.when(has_side[side])
            def _():
                grad_col[1 - side][h].wait_recv()
                out[:, 0, tile_rows[h], at] += grad_cols[1 - side, h]

    for h in range(2):
        for k in range(2):
            tile[k][h].wait_send()
    for k in range(2):
        row_own[k].wait_send()
        row_other[k].wait_send()
        for core in range(2):
            grad_row[core][k].wait_send()

    @pl.when(has_left)
    def _():
        row_left_other.wait_send()
        row_left_own.wait_send()
        for h in range(2):
            leftward[h].wait_send()
            grad_col[0][h].wait_send()

    @pl.when(has_right)
    def _():
        row_right_other.wait_send()
        row_right_own.wait_send()
        for h in range(2):
            rightward[h].wait_send()
            relay_right[h].wait_send()
            relay_beam[h].wait_send()
            grad_col[1][h].wait_send()


def body(cols, transmission, probe_field, propagator, intensities, positions, live_slots):
    anywhere = pl.BlockSpec(memory_space=pl.ANY)
    scalars = pl.BlockSpec(memory_space=pltpu.SMEM)
    plane = (2, SIDE, SIDE)
    stacked = (2, 2 * SIDE, SIDE)
    return pl.pallas_call(
        functools.partial(kernel, cols),
        out_shape=jax.ShapeDtypeStruct((2, 1, SIDE, SIDE), F32),
        in_specs=[scalars, scalars] + [anywhere] * 5,
        out_specs=pl.BlockSpec(memory_space=pltpu.VMEM),
        scratch_shapes=[
            pltpu.VMEM((2, 4, 2, 3 * HALF, HALF), F32),
            pltpu.VMEM(plane, F32),
            pltpu.VMEM(plane, F32),
            pltpu.VMEM(plane, F32),
            pltpu.VMEM(plane, F32),
            pltpu.VMEM((4, 2 * SIDE, 6 * SIDE), BF16),
            pltpu.VMEM((2, SIDE, 6 * SIDE), BF16),
            pltpu.VMEM(stacked, F32),
            pltpu.VMEM(stacked, F32),
            pltpu.VMEM(stacked, F32),
            pltpu.VMEM((2, 5, 2, 4 * HALF, HALF), F32),
            pltpu.VMEM((2, 2, 2, 3 * HALF, HALF), F32),
            pltpu.VMEM((2, 2, 2, HALF, HALF), F32),
            pltpu.VMEM((2, 2, 2, HALF, HALF), F32),
            pltpu.SemaphoreType.DMA((6,)),
            pltpu.SemaphoreType.DMA((COPIES,)),
            pltpu.SemaphoreType.DMA((COPIES,)),
        ],
        compiler_params=pltpu.CompilerParams(
            collective_id=0, has_side_effects=True, vmem_limit_bytes=48 * 1024 * 1024
        ),
    )(
        positions,
        live_slots,
        transmission,
        probe_field,
        propagator,
        jnp.asarray(transform_table(SIDE)),
        intensities,
    )


def solution(mesh):
    return jax.shard_map(
        functools.partial(body, mesh.shape["col"]),
        mesh=mesh,
        in_specs=(
            P(None, "beam", "row", "col"),
            P(),
            P(),
            P(("row", "col"), None, None),
            P(("row", "col"), None),
            P(("row", "col")),
        ),
        out_specs=P(None, "beam", "row", "col"),
        check_vma=False,
    )
```

profile of v0, /device:TPU:156, one launch (start us, length us, event | category | flops | bytes accessed | tf_op | source)
XLA Modules:
  0.0 60.6 jit_solution(7436391190410586999)
XLA Ops:
  0.0 0.0 copy-start
  0.0 1.0 %copy-done = f32[2,1,256,256]{3,2,1,0:T(8,128)S(1)} copy-done((f32[2,1,256,256]{3,2,1,0:T(8,128)S(1)}, f32[2,1,256,256]{3,2,1,0:T(8,128)}, u32[]{:S(2)}) %copy-start) | copy-done | bytes 524312
  1.0 0.0 copy-start.1
  1.0 1.0 %copy-done.1 = f32[2,256,256]{2,1,0:T(8,128)S(1)} copy-done((f32[2,256,256]{2,1,0:T(8,128)S(1)}, f32[2,256,256]{2,1,0:T(8,128)}, u32[]{:S(2)}) %copy-start.1) | copy-done | bytes 524312
  2.1 0.0 copy-start.2
  2.1 1.0 %copy-done.2 = f32[2,256,256]{2,1,0:T(8,128)S(1)} copy-done((f32[2,256,256]{2,1,0:T(8,128)S(1)}, f32[2,256,256]{2,1,0:T(8,128)}, u32[]{:S(2)}) %copy-start.2) | copy-done | bytes 524312
  3.1 0.0 copy-start.3
  3.1 1.0 %copy-done.3 = f32[2,256,256]{2,1,0:T(8,128)S(1)} copy-done((f32[2,256,256]{2,1,0:T(8,128)S(1)}, f32[2,256,256]{2,1,0:T(8,128)}, u32[]{:S(2)}) %copy-start.3) | copy-done | bytes 524312
  4.2 0.0 copy-start.4
  4.2 1.0 %copy-done.4 = f32[2,256,256]{2,1,0:T(8,128)S(1)} copy-done((f32[2,256,256]{2,1,0:T(8,128)S(1)}, f32[2,256,256]{2,1,0:T(8,128)}, u32[]{:S(2)}) %copy-start.4) | copy-done | bytes 524312
  5.2 0.0 copy-start.5
  5.2 0.7 %copy-done.5 = s32[2,2]{1,0:T(2,128)S(1)} copy-done((s32[2,2]{1,0:T(2,128)S(1)}, s32[2,2]{1,0:T(2,128)}, u32[]{:S(2)}) %copy-start.5) | copy-done | bytes 40
  5.9 0.0 copy-start.6
  5.9 0.7 %copy-done.6 = s32[2]{0:T(128)S(1)} copy-done((s32[2]{0:T(128)S(1)}, s32[2]{0:T(128)}, u32[]{:S(2)}) %copy-start.6) | copy-done | bytes 32
  6.5 53.3 %shard_map.73 = f32[2,1,256,256]{3,2,1,0:T(8,128)S(1)} custom-call(s32[2,2]{1,0:T(2,128)S(1)} %copy-done.5, s32[2]{0:T(128)S(1)} %copy-done.6, f32[2,1,256,256]{3,2,1,0:T(8,128)S(1)} %copy-done, f32[2,256,256]{2,1,0:T(8,128)S(1)} %copy-done.1, f32[2,256,256]{2,1,0:T(8,128)S(1)} %copy-done.2, f32[2,256,256]{2,1,0:T(8,128)S(1)} %copy-done.4, ...), custom_call_target="tpu_custom_call" | custom-call | tf_op jit(solution)/shard_map/pallas_call | solution.py:435
  59.8 0.8 %copy.9 = f32[2,1,256,256]{3,2,1,0:T(8,128)} copy(f32[2,1,256,256]{3,2,1,0:T(8,128)S(1)} %shard_map.73) | data formatting | bytes 1048576
Async XLA Ops:
  0.0 1.0 %copy-start = (f32[2,1,256,256]{3,2,1,0:T(8,128)S(1)}, f32[2,1,256,256]{3,2,1,0:T(8,128)}, u32[]{:S(2)}) copy-start(f32[2,1,256,256]{3,2,1,0:T(8,128)} %trans.1) | copy-start | bytes 1572868
  1.0 1.0 %copy-start.1 = (f32[2,256,256]{2,1,0:T(8,128)S(1)}, f32[2,256,256]{2,1,0:T(8,128)}, u32[]{:S(2)}) copy-start(f32[2,256,256]{2,1,0:T(8,128)} %probe_hbm.1) | copy-start | bytes 1572868
  2.1 1.0 %copy-start.2 = (f32[2,256,256]{2,1,0:T(8,128)S(1)}, f32[2,256,256]{2,1,0:T(8,128)}, u32[]{:S(2)}) copy-start(f32[2,256,256]{2,1,0:T(8,128)} %prop_hbm.1) | copy-start | bytes 1572868
  3.1 1.0 %copy-start.3 = (f32[2,256,256]{2,1,0:T(8,128)S(1)}, f32[2,256,256]{2,1,0:T(8,128)}, u32[]{:S(2)}) copy-start(f32[2,256,256]{2,1,0:T(8,128)} %intens_hbm.1) | copy-start | bytes 1572868
  4.2 1.0 %copy-start.4 = (f32[2,256,256]{2,1,0:T(8,128)S(1)}, f32[2,256,256]{2,1,0:T(8,128)}, u32[]{:S(2)}) copy-start(f32[2,256,256]{2,1,0:T(8,128)} %constant.2.clone.table_hbm) | copy-start | bytes 1572868
  5.2 0.7 %copy-start.5 = (s32[2,2]{1,0:T(2,128)S(1)}, s32[2,2]{1,0:T(2,128)}, u32[]{:S(2)}) copy-start(s32[2,2]{1,0:T(2,128)} %pos.1) | copy-start | bytes 52
  5.9 0.7 %copy-start.6 = (s32[2]{0:T(128)S(1)}, s32[2]{0:T(128)}, u32[]{:S(2)}) copy-start(s32[2]{0:T(128)} %live.1) | copy-start | bytes 28
where the time goes:
time: 61 us; the launch traced here: 60.6 us
  Pallas kernels  53.3 us (87%)
  local copies, waits for them, and re-layouts  7.33 us (12%)
    pallas_call x1, Pallas kernels, body(): pl.pallas_call(functools.partial(kernel, cols), out_shape=jax.ShapeDtypeS...  53.3 us
    unnamed x15, local copies, waits for them, and re-layouts  7.33 us

commit v1 on v0

--- a/solution.py
+++ b/solution.py
@@ -49,14 +49,16 @@
 
 def kernel(
     cols,
-    pos,
-    live,
+    pos_hbm,
+    live_hbm,
     trans,
     probe_hbm,
     prop_hbm,
     table_hbm,
     intens_hbm,
     out,
+    pos,
+    live,
     ext,
     probe,
     prop,
@@ -109,7 +111,7 @@
         for k in range(2)
     ]
     for at, (source, target) in enumerate(
-        ((prop_hbm, prop), (table_hbm, table), (probe_hbm, probe), (intens_hbm, intens))
+        ((prop_hbm, prop), (table_hbm, table), (probe_hbm, probe), (intens_hbm, intens), (pos_hbm, pos), (live_hbm, live))
     ):
         locals_.append(pltpu.make_async_copy(source, target, local_sem.at[2 + at]))
     for copy in locals_:
@@ -428,16 +430,17 @@
 
 
 def body(cols, transmission, probe_field, propagator, intensities, positions, live_slots):
-    anywhere = pl.BlockSpec(memory_space=pl.ANY)
-    scalars = pl.BlockSpec(memory_space=pltpu.SMEM)
+    in_hbm = pl.BlockSpec(memory_space=pltpu.HBM)
     plane = (2, SIDE, SIDE)
     stacked = (2, 2 * SIDE, SIDE)
     return pl.pallas_call(
         functools.partial(kernel, cols),
         out_shape=jax.ShapeDtypeStruct((2, 1, SIDE, SIDE), F32),
-        in_specs=[scalars, scalars] + [anywhere] * 5,
+        in_specs=[in_hbm] * 7,
         out_specs=pl.BlockSpec(memory_space=pltpu.VMEM),
         scratch_shapes=[
+            pltpu.SMEM((2, 2), jnp.int32),
+            pltpu.SMEM((2,), jnp.int32),
             pltpu.VMEM((2, 4, 2, 3 * HALF, HALF), F32),
             pltpu.VMEM(plane, F32),
             pltpu.VMEM(plane, F32),
@@ -452,12 +455,12 @@
             pltpu.VMEM((2, 2, 2, 3 * HALF, HALF), F32),
             pltpu.VMEM((2, 2, 2, HALF, HALF), F32),
             pltpu.VMEM((2, 2, 2, HALF, HALF), F32),
-            pltpu.SemaphoreType.DMA((6,)),
+            pltpu.SemaphoreType.DMA((8,)),
             pltpu.SemaphoreType.DMA((COPIES,)),
             pltpu.SemaphoreType.DMA((COPIES,)),
         ],
         compiler_params=pltpu.CompilerParams(
-            collective_id=0, has_side_effects=True, vmem_limit_bytes=48 * 1024 * 1024
+            collective_id=0, has_side_effects=True, vmem_limit_bytes=60 * 1024 * 1024
         ),
     )(
         positions,

time: 61 us -> 55.8 us (0.915)
  local copies, waits for them, and re-layouts: 7.33 us -> 1.87 us
    unnamed x15 -> x1, local copies, waits for them, and re-layouts: 7.33 us -> 1.87 us
where the time goes in v1:
time: 55.8 us; the launch traced here: 55.6 us
  Pallas kernels  53.7 us (96%)
  local copies, waits for them, and re-layouts  1.87 us (3%)
    pallas_call x1, Pallas kernels, body(): pl.pallas_call(functools.partial(kernel, cols), out_shape=jax.ShapeDtypeS...  53.7 us
    unnamed x1, local copies, waits for them, and re-layouts  1.87 us

profile of v1, /device:TPU:156, one launch (start us, length us, event | category | flops | bytes accessed | tf_op | source)
XLA Modules:
  0.0 55.6 jit_solution(3768133743745419502)
XLA Ops:
  0.0 53.7 %shard_map.73 = f32[2,1,256,256]{3,2,1,0:T(8,128)} custom-call(s32[2,2]{1,0:T(2,128)} %pos_hbm.1, s32[2]{0:T(128)} %live_hbm.1, f32[2,1,256,256]{3,2,1,0:T(8,128)} %trans.1, f32[2,256,256]{2,1,0:T(8,128)} %probe_hbm.1, f32[2,256,256]{2,1,0:T(8,128)} %prop_hbm.1, f32[2,256,256]{2,1,0:T(8,128)} %constant.2.clone.table_hbm, f32[2,256,256]{2,1,0:T(8,128)} %intens_hbm.1), custom_call_target="tpu_custom_call" | custom-call | tf_op jit(solution)/shard_map/pallas_call | solution.py:436
  53.7 1.9 %copy.9 = f32[2,1,256,256]{3,2,1,0:T(8,128)} copy(f32[2,1,256,256]{3,2,1,0:T(8,128)} %shard_map.73) | data formatting | bytes 1048576

commit v2 on v1

v2 whole, which is shorter than its diff:
```python
import functools

import jax
import jax.numpy as jnp
import numpy as np
from jax import lax
from jax.experimental import pallas as pl
from jax.experimental.pallas import tpu as pltpu
from jax.sharding import PartitionSpec as P

MESH = pl.DeviceIdType.MESH
SIDE = 256
HALF = 128
F32 = jnp.float32
BF16 = jnp.bfloat16

TILE = 0
LEFTWARD = 4
RIGHTWARD = 6
RELAY_RIGHT = 8
RELAY_BEAM = 10
ROW = 12
GRAD_ROW = 20
GRAD_COL = 24
COPIES = 28


def transform_table(side):
    counter = np.arange(side)
    angles = 2.0 * np.pi / side * (counter[:, None] * counter[None, :] % side)
    return np.stack([np.cos(angles), -np.sin(angles)]).astype(np.float32) / np.float32(np.sqrt(side))


def split(value):
    high = value.astype(BF16)
    return high, (value - high.astype(F32)).astype(BF16)


def put_operator(operators, at, real, imag, scale):
    real, imag = real * scale, imag * scale
    for which, value in enumerate((real, imag, real + imag)):
        high, low = split(value)
        for block, part in enumerate((high, high, low)):
            operators[at, which, :, block * SIDE : (block + 1) * SIDE] = part


def kernel(
    cols,
    pos_hbm,
    live_hbm,
    trans,
    probe_hbm,
    prop_hbm,
    table_hbm,
    intens_hbm,
    core_out,
    halo_out,
    pos,
    live,
    ext,
    whole,
    probe,
    prop,
    table,
    intens,
    operators,
    parts,
    wave,
    psi,
    window,
    pad,
    grad,
    grad_rows,
    core,
    zeros,
    local_sem,
    send_sem,
    recv_sem,
):
    beam, row, col = lax.axis_index("beam"), lax.axis_index("row"), lax.axis_index("col")
    other = 1 - beam
    first_slice, second_slice = beam == 0, beam == 1
    has_left, has_right = col > 0, col < cols - 1
    partner = (other, row, col)
    sibling = (beam, 1 - row, col)
    left = (other, row, jnp.maximum(col - 1, 0))
    right = (other, row, jnp.minimum(col + 1, cols - 1))

    barrier = pltpu.get_barrier_semaphore()

    def greet(peer):
        pl.semaphore_signal(barrier, inc=1, device_id=peer, device_id_type=MESH)

    greet(partner)
    greet(sibling)
    pl.when(has_left)(lambda: greet(left))
    pl.when(has_right)(lambda: greet(right))

    def rows(start):
        return pl.ds(pl.multiple_of(start, HALF), HALF)

    tile_rows = (rows(HALF * (1 - row)), rows(HALF * row))
    ext_rows = (rows(jnp.int32(HALF)), rows(2 * HALF * row))
    sibling_rows = rows(2 * HALF * row)

    locals_ = [
        pltpu.make_async_copy(
            trans.at[:, 0, :, pl.ds(HALF * k, HALF)],
            ext.at[beam, 1 + k, :, pl.ds(pl.multiple_of(HALF * row, HALF), SIDE), :],
            local_sem.at[k],
        )
        for k in range(2)
    ]
    for at, (source, target) in enumerate(
        ((prop_hbm, prop), (table_hbm, table), (probe_hbm, probe), (intens_hbm, intens), (pos_hbm, pos), (live_hbm, live))
    ):
        locals_.append(pltpu.make_async_copy(source, target, local_sem.at[2 + at]))
    for copy in locals_:
        copy.start()

    def remote(at, source, target, peer):
        return pltpu.make_async_remote_copy(
            src_ref=source,
            dst_ref=target,
            send_sem=send_sem.at[at],
            recv_sem=recv_sem.at[at],
            device_id=peer,
            device_id_type=MESH,
        )

    def own(k, h):
        return trans.at[:, 0, tile_rows[h], pl.ds(HALF * k, HALF)]

    def block(of, k, h):
        return ext.at[of, k, :, ext_rows[h], :]

    tile = [[remote(TILE + 2 * k + h, own(k, h), block(beam, 1 + k, h), partner) for h in range(2)] for k in range(2)]
    leftward = [remote(LEFTWARD + h, own(0, h), block(beam, 3, h), left) for h in range(2)]
    rightward = [remote(RIGHTWARD + h, own(1, h), block(beam, 0, h), right) for h in range(2)]
    relay_right = [remote(RELAY_RIGHT + h, block(other, 2, h), block(other, 0, h), right) for h in range(2)]
    relay_beam = [remote(RELAY_BEAM + h, block(other, 3, h), block(other, 3, h), partner) for h in range(2)]

    def to_sibling(at, of, k, source=None):
        return remote(
            ROW + at, block(of, k, 0) if source is None else source, ext.at[of, k, :, sibling_rows, :], sibling
        )

    row_own = [to_sibling(k, beam, 1 + k, own(k, 0)) for k in range(2)]
    row_other = [to_sibling(2 + k, other, 1 + k) for k in range(2)]
    row_left_other = to_sibling(4, other, 0)
    row_left_own = to_sibling(5, beam, 0)
    row_right_other = to_sibling(6, other, 3)
    row_right_own = to_sibling(7, beam, 3)

    pl.semaphore_wait(barrier, 2 + jnp.where(has_left, 1, 0) + jnp.where(has_right, 1, 0))

    for h in range(2):
        tile[1][h].start()
        pl.when(has_left)(leftward[h].start)
    for k in range(2):
        row_own[k].start()

    def send_rest(h):
        tile[0][h].start()
        pl.when(has_right)(rightward[h].start)

    def send_relays(h):
        tile[1][h].wait_recv()
        pl.when(has_right)(relay_right[h].start)
        if h == 0:
            row_other[1].start()

        @pl.when(has_right)
        def _():
            leftward[h].wait_recv()
            relay_beam[h].start()
            if h == 0:
                row_right_other.start()

    def rest_sent(h):
        tile[0][h].wait_send()
        pl.when(has_right)(rightward[h].wait_send)

    def relays_sent(h):
        @pl.when(has_right)
        def _():
            relay_right[h].wait_send()
            relay_beam[h].wait_send()

    def second(h):
        tile[1][h].wait_send()
        pl.when(has_left)(leftward[h].wait_send)
        pl.when(first_slice)(functools.partial(send_rest, h))
        pl.when(second_slice)(functools.partial(send_relays, h))

    def third(h):
        @pl.when(first_slice)
        def _():
            rest_sent(h)
            send_relays(h)

        @pl.when(second_slice)
        def _():
            relays_sent(h)
            send_rest(h)

    def own_edges():
        @pl.when(has_left)
        def _():
            relay_right[0].wait_recv()
            row_left_own.start()

        @pl.when(has_right)
        def _():
            relay_beam[0].wait_recv()
            row_right_own.start()

    def own_rest():
        for k in range(2):
            row_own[k].wait_recv()

        @pl.when(has_left)
        def _():
            relay_right[1].wait_recv()
            row_left_own.wait_recv()

        @pl.when(has_right)
        def _():
            relay_beam[1].wait_recv()
            row_right_own.wait_recv()

    def other_edges():
        tile[0][0].wait_recv()
        row_other[0].start()

        @pl.when(has_left)
        def _():
            rightward[0].wait_recv()
            row_left_other.start()

    def other_rest():
        tile[0][1].wait_recv()
        for k in range(2):
            row_other[k].wait_recv()

        @pl.when(has_left)
        def _():
            rightward[1].wait_recv()
            row_left_other.wait_recv()

        pl.when(has_right)(row_right_other.wait_recv)

    for copy in locals_:
        copy.wait()
    put_operator(operators, 0, prop[0], prop[1], 0.5)
    second(0)
    put_operator(operators, 1, prop[0].T, -prop[1].T, 0.5)
    side_zero = jnp.zeros((2, 2, 3 * HALF, HALF), F32)

    @pl.when(jnp.logical_not(has_left))
    def _():
        ext[:, 0] = side_zero

    @pl.when(jnp.logical_not(has_right))
    def _():
        ext[:, 3] = side_zero

    second(1)
    put_operator(operators, 2, table[0], table[1], 2.0)
    put_operator(operators, 3, table[0], -table[1], 1.0)
    zeros[...] = jnp.zeros_like(zeros)
    no_side = (jnp.logical_not(has_left), jnp.logical_not(has_right))
    no_halo = [
        pltpu.make_async_copy(zeros, halo_out.at[:, 0, :, pl.ds(HALF * side, HALF)], local_sem.at[8])
        for side in range(2)
    ]
    for side in range(2):
        pl.when(no_side[side])(no_halo[side].start)
    edge = jnp.zeros((2, 4 * HALF, HALF), F32)
    strip = jnp.zeros((2, HALF, HALF), F32)
    for of in range(2):
        for slot in range(2):
            pad[of, slot, 0] = edge
            pad[of, slot, 4] = edge
            for k in range(1, 4):
                pad[of, slot, k, :, :HALF] = strip
                pad[of, slot, k, :, 3 * HALF :] = strip
    third(0)
    pl.when(first_slice)(own_edges)
    pl.when(second_slice)(other_edges)
    third(1)
    pl.when(first_slice)(own_rest)
    pl.when(second_slice)(other_rest)

    row_at = [jnp.clip(pos[slot, 0] - HALF - HALF * row, 0, HALF) for slot in range(2)]
    col_at = [jnp.clip(pos[slot, 1] - SIDE * col, 0, SIDE - 1) for slot in range(2)]
    block_at = [at // HALF for at in col_at]
    lane_at = [at % HALF for at in col_at]
    lanes = lax.broadcasted_iota(jnp.int32, (SIDE, HALF), 1)

    for k in range(4):
        whole[k] = ext[0, k]

    def footprint(of, slot, part):
        back = lax.rem(HALF - lane_at[slot], HALF)
        turned = [
            pltpu.roll(of[block_at[slot] + j, part, pl.ds(row_at[slot], SIDE), :], back, 1) for j in range(3)
        ]
        near = lanes < HALF - lane_at[slot]
        return [jnp.where(near, turned[j], turned[j + 1]) for j in range(2)]

    real, imag = slice(0, SIDE), slice(SIDE, 2 * SIDE)

    def spread(operator):
        for _ in range(2):
            for slot in range(2):
                wave_real, wave_imag = wave[slot, real], wave[slot, imag]
                for which, value in enumerate((wave_real, wave_imag, 0.5 * wave_real + 0.5 * wave_imag)):
                    high, low = split(value)
                    for at, part in enumerate((high, low, high)):
                        parts[slot, which, :, at * SIDE : (at + 1) * SIDE] = part
                a, b, c = (
                    lax.dot_general(
                        operators[operator, which],
                        parts[slot, which],
                        (((1,), (1,)), ((), ())),
                        preferred_element_type=F32,
                    )
                    for which in range(3)
                )
                wave[slot, real] = a - b
                wave[slot, imag] = (c - a) + (c - b)


    for slot in range(2):
        window_real, window_imag = footprint(whole, slot, 0), footprint(whole, slot, 1)
        for j in range(2):
            at = slice(j * HALF, (j + 1) * HALF)
            probe_real, probe_imag = probe[0, :, at], probe[1, :, at]
            wave[slot, real, at] = window_real[j] * probe_real - window_imag[j] * probe_imag
            wave[slot, imag, at] = window_real[j] * probe_imag + window_imag[j] * probe_real
    spread(0)

    @pl.when(first_slice)
    def _():
        other_edges()
        other_rest()

    @pl.when(second_slice)
    def _():
        own_edges()
        own_rest()

    for slot in range(2):
        window_real, window_imag = footprint(ext.at[1], slot, 0), footprint(ext.at[1], slot, 1)
        for j in range(2):
            at = slice(j * HALF, (j + 1) * HALF)
            wave_real, wave_imag = 4.0 * wave[slot, real, at], 4.0 * wave[slot, imag, at]
            psi[slot, real, at], psi[slot, imag, at] = wave_real, wave_imag
            window[slot, real, at], window[slot, imag, at] = window_real[j], window_imag[j]
            wave[slot, real, at] = window_real[j] * wave_real - window_imag[j] * wave_imag
            wave[slot, imag, at] = window_real[j] * wave_imag + window_imag[j] * wave_real
    spread(0)
    spread(2)
    for slot in range(2):
        far_real, far_imag = wave[slot, real], wave[slot, imag]
        weight = live[slot].astype(F32)
        residual = weight * (far_real * far_real + far_imag * far_imag - intens[slot])
        wave[slot, real] = residual * far_real
        wave[slot, imag] = residual * far_imag
    spread(3)
    spread(1)

    middle = slice(HALF, 3 * HALF)

    def place(of, slot, part, pieces):
        turned = [pltpu.roll(piece, lane_at[slot], 1) for piece in pieces]
        inside = lanes >= lane_at[slot]
        zero = jnp.zeros_like(turned[0])
        pad[of, slot, 1, part, middle] = jnp.where(inside, turned[0], zero)
        pad[of, slot, 2, part, middle] = jnp.where(inside, turned[1], turned[0])
        pad[of, slot, 3, part, middle] = jnp.where(inside, zero, turned[1])

    def collect(of, k, part):
        terms = [
            pad[of, slot, k + 1 - block_at[slot], part, pl.ds(HALF - row_at[slot], 3 * HALF), :] for slot in range(2)
        ]
        return terms[0] + terms[1]

    def gradient(of, slot, lit_real, lit_imag):
        pieces = ([], [])
        for j in range(2):
            at = slice(j * HALF, (j + 1) * HALF)
            back_real, back_imag = 4.0 * wave[slot, real, at], 4.0 * wave[slot, imag, at]
            first, second = lit_real(at), lit_imag(at)
            pieces[0].append(first * back_real + second * back_imag)
            pieces[1].append(first * back_imag - second * back_real)
        place(of, slot, 0, pieces[0])
        place(of, slot, 1, pieces[1])

    away_rows = rows(2 * HALF * (1 - row))
    grad_row = [
        [
            remote(
                GRAD_ROW + 2 * kind + side, grad.at[kind, side, :, away_rows, :], grad_rows.at[kind, side], sibling
            )
            for side in range(2)
        ]
        for kind in range(2)
    ]
    grad_col = [
        [
            remote(
                GRAD_COL + 2 * side + h,
                grad.at[0, side, :, ext_rows[h], :],
                halo_out.at[:, 0, tile_rows[h], pl.ds(HALF * (1 - side), HALF)],
                right if side else left,
            )
            for h in range(2)
        ]
        for side in range(2)
    ]
    has_side = (has_left, has_right)

    def send_halo(of):
        for side in range(2):
            for part in range(2):
                grad[0, side, part] = collect(of, 3 * side, part)
            grad_row[0][side].start()
            pl.when(has_side[side])(grad_col[side][1].start)

    for slot in range(2):
        gradient(1, slot, lambda at: psi[slot, real, at], lambda at: psi[slot, imag, at])
        back_real, back_imag = 4.0 * wave[slot, real], 4.0 * wave[slot, imag]
        window_real, window_imag = window[slot, real], window[slot, imag]
        wave[slot, real] = window_real * back_real + window_imag * back_imag
        wave[slot, imag] = window_real * back_imag - window_imag * back_real
    pl.when(first_slice)(functools.partial(send_halo, 1))
    spread(1)
    for slot in range(2):
        gradient(0, slot, lambda at: probe[0, :, at], lambda at: probe[1, :, at])
    pl.when(second_slice)(functools.partial(send_halo, 0))
    for side in range(2):
        grad_row[0][side].wait_recv()

        @pl.when(has_side[side])
        def _():
            grad[0, side, :, HALF : 2 * HALF] += grad_rows[0, side]
            grad_col[side][0].start()

    for side in range(2):
        for part in range(2):
            grad[1, side, part] = collect(beam, 1 + side, part)
        grad_row[1][side].start()
    for side in range(2):
        at = slice(side * HALF, (side + 1) * HALF)
        core[:, 0, tile_rows[1], at] = grad[1, side, :, ext_rows[1]]
        grad_row[1][side].wait_recv()
        core[:, 0, tile_rows[0], at] = grad[1, side, :, HALF : 2 * HALF] + grad_rows[1, side]
    core_copy = pltpu.make_async_copy(core, core_out, local_sem.at[9])
    core_copy.start()
    for side in range(2):
        pl.when(no_side[side])(no_halo[side].wait)
    core_copy.wait()
    for h in (1, 0):
        for side in range(2):
            pl.when(has_side[side])(grad_col[1 - side][h].wait_recv)

    for h in range(2):
        pl.when(first_slice)(functools.partial(relays_sent, h))
        pl.when(second_slice)(functools.partial(rest_sent, h))
    for k in range(2):
        row_own[k].wait_send()
        row_other[k].wait_send()
        for kind in range(2):
            grad_row[kind][k].wait_send()

    @pl.when(has_left)
    def _():
        row_left_other.wait_send()
        row_left_own.wait_send()
        for h in range(2):
            grad_col[0][h].wait_send()

    @pl.when(has_right)
    def _():
        row_right_other.wait_send()
        row_right_own.wait_send()
        for h in range(2):
            grad_col[1][h].wait_send()


def body(cols, transmission, probe_field, propagator, intensities, positions, live_slots):
    in_hbm = pl.BlockSpec(memory_space=pltpu.HBM)
    plane = (2, SIDE, SIDE)
    stacked = (2, 2 * SIDE, SIDE)
    tile = jax.ShapeDtypeStruct((2, 1, SIDE, SIDE), F32)
    own, halo = pl.pallas_call(
        functools.partial(kernel, cols),
        out_shape=(tile, tile),
        in_specs=[in_hbm] * 7,
        out_specs=(in_hbm, in_hbm),
        scratch_shapes=[
            pltpu.SMEM((2, 2), jnp.int32),
            pltpu.SMEM((2,), jnp.int32),
            pltpu.VMEM((2, 4, 2, 3 * HALF, HALF), F32),
            pltpu.VMEM((4, 2, 3 * HALF, HALF), F32),
            pltpu.VMEM(plane, F32),
            pltpu.VMEM(plane, F32),
            pltpu.VMEM(plane, F32),
            pltpu.VMEM(plane, F32),
            pltpu.VMEM((4, 3, SIDE, 3 * SIDE), BF16),
            pltpu.VMEM((2, 3, SIDE, 3 * SIDE), BF16),
            pltpu.VMEM(stacked, F32),
            pltpu.VMEM(stacked, F32),
            pltpu.VMEM(stacked, F32),
            pltpu.VMEM((2, 2, 5, 2, 4 * HALF, HALF), F32),
            pltpu.VMEM((2, 2, 2, 3 * HALF, HALF), F32),
            pltpu.VMEM((2, 2, 2, HALF, HALF), F32),
            pltpu.VMEM((2, 1, SIDE, SIDE), F32),
            pltpu.VMEM((2, SIDE, HALF), F32),
            pltpu.SemaphoreType.DMA((10,)),
            pltpu.SemaphoreType.DMA((COPIES,)),
            pltpu.SemaphoreType.DMA((COPIES,)),
        ],
        compiler_params=pltpu.CompilerParams(
            collective_id=0, has_side_effects=True, vmem_limit_bytes=60 * 1024 * 1024
        ),
    )(
        positions,
        live_slots,
        transmission,
        probe_field,
        propagator,
        jnp.asarray(transform_table(SIDE)),
        intensities,
    )
    return own + halo


def solution(mesh):
    return jax.shard_map(
        functools.partial(body, mesh.shape["col"]),
        mesh=mesh,
        in_specs=(
            P(None, "beam", "row", "col"),
            P(),
            P(),
            P(("row", "col"), None, None),
            P(("row", "col"), None),
            P(("row", "col")),
        ),
        out_specs=P(None, "beam", "row", "col"),
        check_vma=False,
    )
```

time: 55.8 us -> 53.4 us (0.957)
  the two profiles are of different devices: /device:TPU:156 before, /device:TPU:126 now
where the time goes in v2:
time: 53.4 us; the launch traced here: 53.3 us
  Pallas kernels  51.2 us (96%)
  other arithmetic  2.06 us (4%)
    pallas_call x1, Pallas kernels, body(): pl.pallas_call(functools.partial(kernel, cols), out_shape=(tile, tile), i...  51.2 us
    add x1, other arithmetic, body(): return own + halo  2.06 us

profile of v2, /device:TPU:126, one launch (start us, length us, event | category | flops | bytes accessed | tf_op | source)
XLA Modules:
  0.0 53.3 jit_solution(5679877858783829713)
XLA Ops:
  0.0 51.2 %shard_map.73 = (f32[2,1,256,256]{3,2,1,0:T(8,128)}, f32[2,1,256,256]{3,2,1,0:T(8,128)}) custom-call(s32[2,2]{1,0:T(2,128)} %pos_hbm.1, s32[2]{0:T(128)} %live_hbm.1, f32[2,1,256,256]{3,2,1,0:T(8,128)} %trans.1, f32[2,256,256]{2,1,0:T(8,128)} %probe_hbm.1, f32[2,256,256]{2,1,0:T(8,128)} %prop_hbm.1, f32[2,256,256]{2,1,0:T(8,128)} %constant.2.clone.table_hbm, ...), custom_call_target="tpu_custom_call" | custom-call | tf_op jit(solution)/shard_map/pallas_call | solution.py:498
  51.2 2.1 %add.3 = f32[2,1,256,256]{3,2,1,0:T(8,128)} add(f32[2,1,256,256]{3,2,1,0:T(8,128)} %get-tuple-element.7, f32[2,1,256,256]{3,2,1,0:T(8,128)} %get-tuple-element.8) | non-fusion elementwise | flops 131072 | bytes 1572864 | tf_op jit(solution)/shard_map/add | solution.py:538

commit v3 on v2

--- a/solution.py
+++ b/solution.py
@@ -118,7 +118,7 @@
     for copy in locals_:
         copy.start()
 
-    def remote(at, source, target, peer):
+    def remote(at, source, target, peer, arrives=None):
         return pltpu.make_async_remote_copy(
             src_ref=source,
             dst_ref=target,
@@ -154,15 +154,17 @@
 
     pl.semaphore_wait(barrier, 2 + jnp.where(has_left, 1, 0) + jnp.where(has_right, 1, 0))
 
+    def send_rest(h):
+        tile[0][h].start()
+        pl.when(has_right)(rightward[h].start)
+
     for h in range(2):
         tile[1][h].start()
         pl.when(has_left)(leftward[h].start)
     for k in range(2):
         row_own[k].start()
-
-    def send_rest(h):
-        tile[0][h].start()
-        pl.when(has_right)(rightward[h].start)
+    for h in range(2):
+        send_rest(h)
 
     def send_relays(h):
         tile[1][h].wait_recv()
@@ -177,33 +179,6 @@
             if h == 0:
                 row_right_other.start()
 
-    def rest_sent(h):
-        tile[0][h].wait_send()
-        pl.when(has_right)(rightward[h].wait_send)
-
-    def relays_sent(h):
-        @pl.when(has_right)
-        def _():
-            relay_right[h].wait_send()
-            relay_beam[h].wait_send()
-
-    def second(h):
-        tile[1][h].wait_send()
-        pl.when(has_left)(leftward[h].wait_send)
-        pl.when(first_slice)(functools.partial(send_rest, h))
-        pl.when(second_slice)(functools.partial(send_relays, h))
-
-    def third(h):
-        @pl.when(first_slice)
-        def _():
-            rest_sent(h)
-            send_relays(h)
-
-        @pl.when(second_slice)
-        def _():
-            relays_sent(h)
-            send_rest(h)
-
     def own_edges():
         @pl.when(has_left)
         def _():
@@ -253,7 +228,7 @@
     for copy in locals_:
         copy.wait()
     put_operator(operators, 0, prop[0], prop[1], 0.5)
-    second(0)
+    send_relays(0)
     put_operator(operators, 1, prop[0].T, -prop[1].T, 0.5)
     side_zero = jnp.zeros((2, 2, 3 * HALF, HALF), F32)
 
@@ -265,7 +240,7 @@
     def _():
         ext[:, 3] = side_zero
 
-    second(1)
+    send_relays(1)
     put_operator(operators, 2, table[0], table[1], 2.0)
     put_operator(operators, 3, table[0], -table[1], 1.0)
     zeros[...] = jnp.zeros_like(zeros)
@@ -285,10 +260,8 @@
             for k in range(1, 4):
                 pad[of, slot, k, :, :HALF] = strip
                 pad[of, slot, k, :, 3 * HALF :] = strip
-    third(0)
     pl.when(first_slice)(own_edges)
     pl.when(second_slice)(other_edges)
-    third(1)
     pl.when(first_slice)(own_rest)
     pl.when(second_slice)(other_rest)
 
@@ -467,8 +440,16 @@
             pl.when(has_side[side])(grad_col[1 - side][h].wait_recv)
 
     for h in range(2):
-        pl.when(first_slice)(functools.partial(relays_sent, h))
-        pl.when(second_slice)(functools.partial(rest_sent, h))
+        tile[1][h].wait_send()
+        tile[0][h].wait_send()
+        pl.when(has_left)(leftward[h].wait_send)
+
+        @pl.when(has_right)
+        def _():
+            rightward[h].wait_send()
+            relay_right[h].wait_send()
+            relay_beam[h].wait_send()
+
     for k in range(2):
         row_own[k].wait_send()
         row_other[k].wait_send()

time: 53.4 us -> 50.8 us (0.951)
  the two profiles are of different devices: /device:TPU:126 before, /device:TPU:159 now
where the time goes in v3:
time: 50.8 us; the launch traced here: 50.7 us
  Pallas kernels  48.6 us (96%)
  other arithmetic  2.06 us (4%)
    pallas_call x1, Pallas kernels, body(): pl.pallas_call(functools.partial(kernel, cols), out_shape=(tile, tile), i...  48.6 us
    add x1, other arithmetic, body(): return own + halo  2.06 us

profile of v3, /device:TPU:159, one launch (start us, length us, event | category | flops | bytes accessed | tf_op | source)
XLA Modules:
  0.0 50.7 jit_solution(13687744888529659900)
XLA Ops:
  0.0 48.6 %shard_map.73 = (f32[2,1,256,256]{3,2,1,0:T(8,128)}, f32[2,1,256,256]{3,2,1,0:T(8,128)}) custom-call(s32[2,2]{1,0:T(2,128)} %pos_hbm.1, s32[2]{0:T(128)} %live_hbm.1, f32[2,1,256,256]{3,2,1,0:T(8,128)} %trans.1, f32[2,256,256]{2,1,0:T(8,128)} %probe_hbm.1, f32[2,256,256]{2,1,0:T(8,128)} %prop_hbm.1, f32[2,256,256]{2,1,0:T(8,128)} %constant.2.clone.table_hbm, ...), custom_call_target="tpu_custom_call" | custom-call | tf_op jit(solution)/shard_map/pallas_call | solution.py:479
  48.6 2.1 %add.3 = f32[2,1,256,256]{3,2,1,0:T(8,128)} add(f32[2,1,256,256]{3,2,1,0:T(8,128)} %get-tuple-element.7, f32[2,1,256,256]{3,2,1,0:T(8,128)} %get-tuple-element.8) | non-fusion elementwise | flops 131072 | bytes 1572864 | tf_op jit(solution)/shard_map/add | solution.py:519

commit v4 on v3

--- a/solution.py
+++ b/solution.py
@@ -20,9 +20,11 @@
 RELAY_RIGHT = 8
 RELAY_BEAM = 10
 ROW = 12
-GRAD_ROW = 20
-GRAD_COL = 24
-COPIES = 28
+SHARE = 20
+GRAD_ROW = 21
+GRAD_COL = 25
+COPIES = 29
+LAYER = 8
 
 
 def transform_table(side):
@@ -81,6 +83,10 @@
     other = 1 - beam
     first_slice, second_slice = beam == 0, beam == 1
     has_left, has_right = col > 0, col < cols - 1
+    shared_here = jnp.logical_and(has_left, lax.rem(col, LAYER) == 0)
+    shared_next = jnp.logical_and(has_right, lax.rem(col, LAYER) == LAYER - 1)
+    relayed_here = (has_left, jnp.logical_and(has_left, jnp.logical_not(shared_here)))
+    relayed_next = (has_right, jnp.logical_and(has_right, jnp.logical_not(shared_next)))
     partner = (other, row, col)
     sibling = (beam, 1 - row, col)
     left = (other, row, jnp.maximum(col - 1, 0))
@@ -138,6 +144,12 @@
     leftward = [remote(LEFTWARD + h, own(0, h), block(beam, 3, h), left) for h in range(2)]
     rightward = [remote(RIGHTWARD + h, own(1, h), block(beam, 0, h), right) for h in range(2)]
     relay_right = [remote(RELAY_RIGHT + h, block(other, 2, h), block(other, 0, h), right) for h in range(2)]
+    quarters = [pl.ds(pl.multiple_of(2 * HALF * row + HALF // 2 * at, HALF // 2), HALF // 2) for at in range(2)]
+    relay_part = remote(
+        RELAY_RIGHT + 1, ext.at[other, 2, :, quarters[0], :], ext.at[other, 0, :, quarters[0], :], right
+    )
+    share_block = ext.at[other, 0, :, quarters[1], :]
+    share = remote(SHARE, share_block, share_block, partner)
     relay_beam = [remote(RELAY_BEAM + h, block(other, 3, h), block(other, 3, h), partner) for h in range(2)]
 
     def to_sibling(at, of, k, source=None):
@@ -154,21 +166,22 @@
 
     pl.semaphore_wait(barrier, 2 + jnp.where(has_left, 1, 0) + jnp.where(has_right, 1, 0))
 
-    def send_rest(h):
-        tile[0][h].start()
-        pl.when(has_right)(rightward[h].start)
-
+    for h in range(2):
+        pl.when(shared_next)(rightward[h].start)
     for h in range(2):
         tile[1][h].start()
         pl.when(has_left)(leftward[h].start)
     for k in range(2):
         row_own[k].start()
     for h in range(2):
-        send_rest(h)
+        tile[0][h].start()
+        pl.when(relayed_next[1])(rightward[h].start)
 
     def send_relays(h):
         tile[1][h].wait_recv()
-        pl.when(has_right)(relay_right[h].start)
+        pl.when(relayed_next[h])(relay_right[h].start)
+        if h == 1:
+            pl.when(shared_next)(relay_part.start)
         if h == 0:
             row_other[1].start()
 
@@ -194,10 +207,10 @@
         for k in range(2):
             row_own[k].wait_recv()
 
-        @pl.when(has_left)
-        def _():
-            relay_right[1].wait_recv()
-            row_left_own.wait_recv()
+        pl.when(relayed_here[1])(relay_right[1].wait_recv)
+        pl.when(shared_here)(relay_part.wait_recv)
+        pl.when(shared_here)(share.wait_recv)
+        pl.when(has_left)(row_left_own.wait_recv)
 
         @pl.when(has_right)
         def _():
@@ -218,10 +231,8 @@
         for k in range(2):
             row_other[k].wait_recv()
 
-        @pl.when(has_left)
-        def _():
-            rightward[1].wait_recv()
-            row_left_other.wait_recv()
+        pl.when(relayed_here[1])(rightward[1].wait_recv)
+        pl.when(has_left)(row_left_other.wait_recv)
 
         pl.when(has_right)(row_right_other.wait_recv)
 
@@ -241,6 +252,12 @@
         ext[:, 3] = side_zero
 
     send_relays(1)
+
+    @pl.when(shared_here)
+    def _():
+        rightward[1].wait_recv()
+        share.start()
+
     put_operator(operators, 2, table[0], table[1], 2.0)
     put_operator(operators, 3, table[0], -table[1], 1.0)
     zeros[...] = jnp.zeros_like(zeros)
@@ -444,12 +461,15 @@
         tile[0][h].wait_send()
         pl.when(has_left)(leftward[h].wait_send)
 
+        pl.when(relayed_next[h])(relay_right[h].wait_send)
+
         @pl.when(has_right)
         def _():
             rightward[h].wait_send()
-            relay_right[h].wait_send()
             relay_beam[h].wait_send()
 
+    pl.when(shared_here)(share.wait_send)
+    pl.when(shared_next)(relay_part.wait_send)
     for k in range(2):
         row_own[k].wait_send()
         row_other[k].wait_send()

time: 50.8 us -> 49.5 us (0.974)
  Pallas kernels: 48.6 us -> 47.3 us
    pallas_call x1, Pallas kernels: 48.6 us -> 47.3 us  [body(): pl.pallas_call(functools.partial(kernel, cols), out_shape=(tile, tile), i...]
where the time goes in v4:
time: 49.5 us; the launch traced here: 49.3 us
  Pallas kernels  47.3 us (96%)
  other arithmetic  2.06 us (4%)
    pallas_call x1, Pallas kernels, body(): pl.pallas_call(functools.partial(kernel, cols), out_shape=(tile, tile), i...  47.3 us
    add x1, other arithmetic, body(): return own + halo  2.06 us

profile of v4, /device:TPU:159, one launch (start us, length us, event | category | flops | bytes accessed | tf_op | source)
XLA Modules:
  0.0 49.3 jit_solution(9357797918042579488)
XLA Ops:
  0.0 47.3 %shard_map.73 = (f32[2,1,256,256]{3,2,1,0:T(8,128)}, f32[2,1,256,256]{3,2,1,0:T(8,128)}) custom-call(s32[2,2]{1,0:T(2,128)} %pos_hbm.1, s32[2]{0:T(128)} %live_hbm.1, f32[2,1,256,256]{3,2,1,0:T(8,128)} %trans.1, f32[2,256,256]{2,1,0:T(8,128)} %probe_hbm.1, f32[2,256,256]{2,1,0:T(8,128)} %prop_hbm.1, f32[2,256,256]{2,1,0:T(8,128)} %constant.2.clone.table_hbm, ...), custom_call_target="tpu_custom_call" | custom-call | tf_op jit(solution)/shard_map/pallas_call | solution.py:499
  47.3 2.1 %add.3 = f32[2,1,256,256]{3,2,1,0:T(8,128)} add(f32[2,1,256,256]{3,2,1,0:T(8,128)} %get-tuple-element.7, f32[2,1,256,256]{3,2,1,0:T(8,128)} %get-tuple-element.8) | non-fusion elementwise | flops 131072 | bytes 1572864 | tf_op jit(solution)/shard_map/add | solution.py:539

commit v5 on v4

--- a/solution.py
+++ b/solution.py
@@ -252,12 +252,6 @@
         ext[:, 3] = side_zero
 
     send_relays(1)
-
-    @pl.when(shared_here)
-    def _():
-        rightward[1].wait_recv()
-        share.start()
-
     put_operator(operators, 2, table[0], table[1], 2.0)
     put_operator(operators, 3, table[0], -table[1], 1.0)
     zeros[...] = jnp.zeros_like(zeros)
@@ -277,6 +271,11 @@
             for k in range(1, 4):
                 pad[of, slot, k, :, :HALF] = strip
                 pad[of, slot, k, :, 3 * HALF :] = strip
+    @pl.when(shared_here)
+    def _():
+        rightward[1].wait_recv()
+        share.start()
+
     pl.when(first_slice)(own_edges)
     pl.when(second_slice)(other_edges)
     pl.when(first_slice)(own_rest)

time: 49.5 us -> 49.4 us (level)
  no operation moved by 1% of the time
where the time goes in v5:
time: 49.4 us; the launch traced here: 49.3 us
  Pallas kernels  47.2 us (96%)
  other arithmetic  2.06 us (4%)
    pallas_call x1, Pallas kernels, body(): pl.pallas_call(functools.partial(kernel, cols), out_shape=(tile, tile), i...  47.2 us
    add x1, other arithmetic, body(): return own + halo  2.06 us

profile of v5, /device:TPU:159, one launch (start us, length us, event | category | flops | bytes accessed | tf_op | source)
XLA Modules:
  0.0 49.3 jit_solution(382489174908404916)
XLA Ops:
  0.0 47.2 %shard_map.73 = (f32[2,1,256,256]{3,2,1,0:T(8,128)}, f32[2,1,256,256]{3,2,1,0:T(8,128)}) custom-call(s32[2,2]{1,0:T(2,128)} %pos_hbm.1, s32[2]{0:T(128)} %live_hbm.1, f32[2,1,256,256]{3,2,1,0:T(8,128)} %trans.1, f32[2,256,256]{2,1,0:T(8,128)} %probe_hbm.1, f32[2,256,256]{2,1,0:T(8,128)} %prop_hbm.1, f32[2,256,256]{2,1,0:T(8,128)} %constant.2.clone.table_hbm, ...), custom_call_target="tpu_custom_call" | custom-call | tf_op jit(solution)/shard_map/pallas_call | solution.py:498
  47.2 2.1 %add.3 = f32[2,1,256,256]{3,2,1,0:T(8,128)} add(f32[2,1,256,256]{3,2,1,0:T(8,128)} %get-tuple-element.7, f32[2,1,256,256]{3,2,1,0:T(8,128)} %get-tuple-element.8) | non-fusion elementwise | flops 131072 | bytes 1572864 | tf_op jit(solution)/shard_map/add | solution.py:538
